TPU v7x, 512 devices: a whole 4x8x8 slice. The times are simulated.
512 devices in a mesh: section: 32 (over z_lo, x, core), tensor: 16 (over z_hi, y).
Axes of the slice: x: 4, y: 8, z: 8 (z_hi: 2, z_lo: 4; z = z_hi * 4 + z_lo), core: 2. Of those that a mesh axis runs over, the one named last changes fastest.
Arguments:
- transit_latents: bfloat16 [32, 256, 512], P('section', None, 'tensor'), may hold values from -6 to 6
- encoded_arrivals: bfloat16 [2, 256, 512], P(None, None, 'tensor'), may hold values from -6 to 6
- arriving_latent_derivative: bfloat16 [32, 256, 512], P('section', None, 'tensor'), may hold values from -6 to 6
- objective_derivative_arrivals: bfloat16 [2, 256, 512], P(None, None, 'tensor'), may hold values from -6 to 6
- kept_inputs: bfloat16 [32, 3, 256, 512], P('section', None, None, 'tensor'), may hold values from -6 to 6
- onward_sequence_labels: int32 [34, 256], replicated, may hold values from 0 to 3, never falling along the last dimension, each value on 1 to 128 neighbouring positions
- reverse_sequence_labels: int32 [34, 256], replicated, may hold values from 0 to 3, never falling along the last dimension, each value on 1 to 128 neighbouring positions
- expander_attn_factors: bfloat16 [32, 512, 12288], P('section', None, 'tensor'), may hold values from -0.25 to 0.25
- outgoing_compressor_factors: bfloat16 [32, 4096, 512], P('section', 'tensor'), may hold values from -0.09375 to 0.09375
Outputs:
- codes_out: bfloat16 [32, 3, 256, 512], P('section', None, None, 'tensor')
- grads_out: bfloat16 [32, 3, 256, 512], P('section', None, None, 'tensor')
- grad_qkv: float32 [32, 512, 12288], P('section', None, 'tensor')
- grad_out: float32 [32, 4096, 512], P('section', 'tensor')
Inputs may be any that keep to these rules, and one draw needn't show every extreme that they name: `onward_sequence_labels`: along each row the ids never fall; a document spans at most 128 tokens, and some document spans exactly that many. `reverse_sequence_labels`: along each row the ids never fall; a document spans at most 128 tokens, and some document spans exactly that many.
All inputs are finite; a program needn't handle non-finite values.
Results may differ from a plain program's by a relative error of at most 0.03.
Values may be sent and summed in bfloat16 or wider, within the bound.
A program may use at most 64 MiB of HBM per device.

v0:
```python
import jax
import jax.numpy as jnp
from jax import lax
from jax.sharding import PartitionSpec as P

HD = 128


attention_score_scale = 8.0
norm_eps = 1e-05
head_eps = 1e-06


def shifted(value, axis, steps):
    count = lax.axis_size(axis)
    leading, last = (max(0, -steps), min(count, count - steps))
    return lax.ppermute(value, axis, [(source, source + steps) for source in range(leading, last)])


def contract_heads(form, left, right):
    return jnp.einsum(form, left, right, preferred_element_type=jnp.float32)


def norm_rows(value_rows, eps):
    factor = lax.rsqrt(jnp.mean(value_rows * value_rows, axis=-1, keepdims=True) + eps)
    return (value_rows * factor, factor)


def norm_back(grad, normed, factor):
    return factor * (grad - normed * jnp.mean(grad * normed, axis=-1, keepdims=True))


def attend(compact_interface_latents, expander_attn_factors, segs, head_entry_width):
    token_row_block = compact_interface_latents.shape[0]
    normed32, row_factor = norm_rows(compact_interface_latents.astype(jnp.float32), norm_eps)
    normed = normed32.astype(jnp.bfloat16)
    packed = jnp.dot(normed, expander_attn_factors, preferred_element_type=jnp.float32).astype(
        jnp.bfloat16
    )
    packed = packed.reshape(token_row_block, -1, 3, head_entry_width)
    query, keys, value_rows = (packed[:, :, 0], packed[:, :, 1], packed[:, :, 2])
    query32, query_factor = norm_rows(query.astype(jnp.float32), head_eps)
    keys32, keys_factor = norm_rows(keys.astype(jnp.float32), head_eps)
    normalized_query = query32.astype(jnp.bfloat16)
    normalized_keys = keys32.astype(jnp.bfloat16)
    score_matrix = contract_heads("ypz,vpz->pyv", normalized_query, normalized_keys) * (
        attention_score_scale / head_entry_width
    )
    position = jnp.arange(token_row_block, dtype=jnp.int32)
    allowed = (position[None, :] <= position[:, None]) & (segs[None, :] == segs[:, None])
    weights = jnp.where(allowed[None], jnp.exp(score_matrix), jnp.float32(0.0))
    probs = weights / jnp.sum(weights, axis=-1, keepdims=True)
    backward_probabilities = probs.astype(jnp.bfloat16)
    mixed_value_rows = (
        contract_heads("gra,agy->rgy", backward_probabilities, value_rows)
        .astype(jnp.bfloat16)
        .reshape(token_row_block, -1)
    )
    return (
        normed32,
        row_factor,
        normed,
        query32,
        query_factor,
        normalized_query,
        keys32,
        keys_factor,
        normalized_keys,
        value_rows,
        probs,
        backward_probabilities,
        mixed_value_rows,
    )


def backward_terms(
    compact_interface_latents,
    grad,
    expander_attn_factors,
    outgoing_compressor_factors,
    segs,
    head_entry_width,
):
    (
        normed32,
        row_factor,
        normed,
        query32,
        query_factor,
        normalized_query,
        keys32,
        keys_factor,
        normalized_keys,
        value_rows,
        probs,
        backward_probabilities,
        mixed_value_rows,
    ) = attend(compact_interface_latents, expander_attn_factors, segs, head_entry_width)
    token_row_block = compact_interface_latents.shape[0]
    grad_wout = jnp.dot(mixed_value_rows.T, grad, preferred_element_type=jnp.float32)
    gradient_mixed_values = jnp.dot(
        grad, outgoing_compressor_factors.T, preferred_element_type=jnp.float32
    ).astype(jnp.bfloat16)
    gradient_mixed_values = gradient_mixed_values.reshape(token_row_block, -1, head_entry_width)
    gradient_probabilities = contract_heads("ypz,vpz->pyv", gradient_mixed_values, value_rows)
    gradient_value_rows = contract_heads(
        "qrp,rqf->pqf", backward_probabilities, gradient_mixed_values
    ).astype(jnp.bfloat16)
    inner = jnp.sum(probs * gradient_probabilities, axis=-1, keepdims=True)
    gradient_score_matrix = (
        probs * (gradient_probabilities - inner) * (attention_score_scale / head_entry_width)
    ).astype(jnp.bfloat16)
    gradient_normed_query = contract_heads("gra,agy->rgy", gradient_score_matrix, normalized_keys)
    gradient_normed_keys = contract_heads("qrp,rqf->pqf", gradient_score_matrix, normalized_query)
    d_query = norm_back(gradient_normed_query, query32, query_factor).astype(jnp.bfloat16)
    d_keys = norm_back(gradient_normed_keys, keys32, keys_factor).astype(jnp.bfloat16)
    d_packed = jnp.stack([d_query, d_keys, gradient_value_rows], axis=2).reshape(
        token_row_block, -1
    )
    grad_wqkv = jnp.dot(normed.T, d_packed, preferred_element_type=jnp.float32)
    d_normed = jnp.dot(d_packed, expander_attn_factors.T, preferred_element_type=jnp.float32)
    return (norm_back(d_normed, normed32, row_factor), grad_wqkv, grad_wout)


def body(
    transit_latents,
    encoded_arrivals,
    arriving_latent_derivative,
    objective_derivative_arrivals,
    kept_inputs,
    onward_sequence_labels,
    reverse_sequence_labels,
    expander_attn_factors,
    outgoing_compressor_factors,
):
    section = lax.axis_index("section")
    sections = lax.axis_size("section")
    rank = lax.axis_index("tensor")
    ticks = kept_inputs.shape[1]
    shard_piece = transit_latents.shape[2]
    weights_qkv = expander_attn_factors[0]
    weights_out = outgoing_compressor_factors[0]
    first = section == 0
    final = section == sections - 1
    codes_full, grads_full, stash_full = (
        lax.all_gather(transit_latents[0], "tensor", axis=1, tiled=True),
        lax.all_gather(arriving_latent_derivative[0], "tensor", axis=1, tiled=True),
        lax.all_gather(kept_inputs[0], "tensor", axis=2, tiled=True),
    )
    feed_full, loss_full = (
        lax.all_gather(encoded_arrivals, "tensor", axis=2, tiled=True),
        lax.all_gather(objective_derivative_arrivals, "tensor", axis=2, tiled=True),
    )
    total_qkv = jnp.zeros(weights_qkv.shape, jnp.float32)
    total_out = jnp.zeros(weights_out.shape, jnp.float32)
    codes_list = []
    grads_list = []
    for tick in range(ticks):
        fseg = lax.dynamic_slice_in_dim(
            onward_sequence_labels, tick - section + sections - 1, 1, 0
        )[0]
        bseg = lax.dynamic_slice_in_dim(reverse_sequence_labels, tick + section, 1, 0)[0]
        mixed_value_rows = attend(codes_full, weights_qkv, fseg, HD)[-1]
        head_term = jnp.dot(mixed_value_rows, weights_out, preferred_element_type=jnp.float32)
        back_term, part_qkv, part_out = backward_terms(
            stash_full[tick], grads_full, weights_qkv, weights_out, bseg, HD
        )
        total_qkv = total_qkv + part_qkv
        total_out = total_out + part_out
        head_total, back_total = (
            lax.psum(head_term.astype(jnp.bfloat16), "tensor").astype(jnp.float32),
            lax.psum(back_term.astype(jnp.bfloat16), "tensor").astype(jnp.float32),
        )
        produced = (codes_full.astype(jnp.float32) + head_total).astype(jnp.bfloat16)
        returned = (grads_full.astype(jnp.float32) + back_total).astype(jnp.bfloat16)
        codes_list.append(lax.dynamic_slice_in_dim(produced, rank * shard_piece, shard_piece, 1))
        grads_list.append(lax.dynamic_slice_in_dim(returned, rank * shard_piece, shard_piece, 1))
        if tick + 1 < ticks:
            arrived = shifted(produced, "section", 1)
            came_back = shifted(returned, "section", -1)
            codes_full = jnp.where(first, feed_full[tick], arrived)
            grads_full = jnp.where(final, loss_full[tick], came_back)
    codes_out = jnp.stack(codes_list, axis=0)[None]
    grads_out = jnp.stack(grads_list, axis=0)[None]
    return (codes_out, grads_out, total_qkv[None], total_out[None])


def solution(mesh):
    in_specs = (
        P("section", None, "tensor"),
        P(None, None, "tensor"),
        P("section", None, "tensor"),
        P(None, None, "tensor"),
        P("section", None, None, "tensor"),
        P(),
        P(),
        P("section", None, "tensor"),
        P("section", "tensor", None),
    )
    out_specs = (
        P("section", None, None, "tensor"),
        P("section", None, None, "tensor"),
        P("section", None, "tensor"),
        P("section", "tensor", None),
    )
    return jax.shard_map(body, mesh=mesh, in_specs=in_specs, out_specs=out_specs, check_vma=False)
```

profile of v0, /device:TPU:2, one launch (start us, length us, event | category | flops | bytes accessed | tf_op | source)
XLA Modules:
  0.0 856.0 jit_solution(9412015653577351168)
XLA Ops:
  8.2 65.1 %all-gather.2 = bf16[1,3,256,512]{2,3,1,0:T(8,128)(2,1)S(1)} all-gather(bf16[1,3,256,32]{2,3,1,0:T(8,128)(2,1)} %param.13), channel_id=4, replica_groups=mesh['section'=32,'tensor'=16] {'tensor'}, dimensions={3}, use_global_device_ids=true | all-gather | bytes 835584 | tf_op jit(solution)/shard_map/all_gather | solution.py:148
  75.1 46.8 %all-gather.1 = bf16[1,256,512]{1,2,0:T(8,128)(2,1)S(1)} all-gather(bf16[1,256,32]{1,2,0:T(8,128)(2,1)S(1)} %copy-done.33), channel_id=3, replica_groups=mesh['section'=32,'tensor'=16] {'tensor'}, dimensions={2}, use_global_device_ids=true | all-gather | bytes 278528 | tf_op jit(solution)/shard_map/all_gather | solution.py:147
  131.4 48.8 %all-gather = bf16[1,256,512]{1,2,0:T(8,128)(2,1)S(1)} all-gather(bf16[1,256,32]{1,2,0:T(8,128)(2,1)S(1)} %copy-done.34), channel_id=2, replica_groups=mesh['section'=32,'tensor'=16] {'tensor'}, dimensions={2}, use_global_device_ids=true | all-gather | bytes 278528 | tf_op jit(solution)/shard_map/all_gather | solution.py:146
  184.6 2.1 fusion.14
  191.3 51.2 %all_gather.19 = bf16[2,256,512]{1,0,2:T(2,128)(2,1)S(1)} all-gather(bf16[2,256,32]{1,0,2:T(2,128)(2,1)S(1)} %copy.167), channel_id=1, replica_groups=mesh['section'=32,'tensor'=16] {'tensor'}, dimensions={2}, use_global_device_ids=true | all-gather | bytes 557056 | tf_op jit(solution)/shard_map/all_gather | solution.py:152
  248.3 51.2 %all_gather.16 = bf16[2,256,512]{1,0,2:T(2,128)(2,1)S(1)} all-gather(bf16[2,256,32]{1,0,2:T(2,128)(2,1)S(1)} %copy.137), channel_id=1, replica_groups=mesh['section'=32,'tensor'=16] {'tensor'}, dimensions={2}, use_global_device_ids=true | all-gather | bytes 557056 | tf_op jit(solution)/shard_map/all_gather | solution.py:151
  311.8 69.9 %all-reduce.11.cloned.1.call-done = (bf16[256,512]{1,0:T(8,128)(2,1)}, bf16[256,512]{1,0:T(8,128)(2,1)}) async-done(((bf16[256,512]{1,0:T(8,128)(2,1)}, bf16[256,512]{1,0:T(8,128)(2,1)}), (bf16[256,512]{1,0:T(8,128)(2,1)}, bf16[256,512]{1,0:T(8,128)(2,1)})) %all-reduce.11.cloned.1.call-update) | async-done | bytes 524304 | tf_op jit(solution)/shard_map/psum | solution.py:171
  386.6 2.6 collective-permute-start
  392.3 2.0 fusion.220
  394.5 2.6 convolution_bitcast_fusion.2
  397.2 3.4 fusion.139
  411.9 2.1 fusion.12
  413.9 2.2 convolution_convert_fusion.19
  420.1 2.1 convolution_add_fusion.1
  422.2 2.3 fusion.237
  424.5 189.5 %all-reduce.9.cloned.1.call-done = (bf16[256,512]{1,0:T(8,128)(2,1)}, bf16[256,512]{1,0:T(8,128)(2,1)}) async-done(((bf16[256,512]{1,0:T(8,128)(2,1)}, bf16[256,512]{1,0:T(8,128)(2,1)}), (bf16[256,512]{1,0:T(8,128)(2,1)}, bf16[256,512]{1,0:T(8,128)(2,1)})) %all-reduce.9.cloned.1.call-update) | async-done | bytes 524304 | tf_op jit(solution)/shard_map/psum | solution.py:171
  619.5 2.4 collective-permute-start.1
  626.9 2.5 convolution_bitcast_fusion
  629.4 3.3 fusion.149
  644.1 2.1 fusion.10
  646.1 2.2 convolution_convert_fusion.18
  653.2 2.1 fusion.24
  655.3 3.1 add_bitcast_fusion
  658.4 187.6 %all-reduce.7.cloned.1.call-done = (bf16[256,512]{1,0:T(8,128)(2,1)}, bf16[256,512]{1,0:T(8,128)(2,1)}) async-done(((bf16[256,512]{1,0:T(8,128)(2,1)}, bf16[256,512]{1,0:T(8,128)(2,1)}), (bf16[256,512]{1,0:T(8,128)(2,1)}, bf16[256,512]{1,0:T(8,128)(2,1)})) %all-reduce.7.cloned.1.call-update) | async-done | bytes 524304 | tf_op jit(solution)/shard_map/psum | solution.py:171
  (224 shorter events, 92.4 us)
Async XLA Ops:
  7.2 67.2 %copy-start = (bf16[1,512,768]{2,1,0:T(8,128)(2,1)S(1)}, bf16[1,512,768]{2,1,0:T(8,128)(2,1)}, u32[]{:S(2)}) copy-start(bf16[1,512,768]{2,1,0:T(8,128)(2,1)} %param.16) | copy-start | bytes 2359300
  7.2 374.6 %all-reduce.11.cloned.1.call-start = ((), (), s32[]{:S(2)}) async-start(), calls=%async_computation.2 | async-start | bytes 1048576 | tf_op jit(solution)/shard_map/psum | solution.py:171
  74.2 47.6 %copy-start.1 = (bf16[1,256,512]{2,1,0:T(8,128)(2,1)S(1)}, bf16[1,256,512]{2,1,0:T(8,128)(2,1)}, u32[]{:S(2)}) copy-start(bf16[1,256,512]{2,1,0:T(8,128)(2,1)} %param.17) | copy-start | bytes 786436
  127.5 3.9 copy-start.34
  180.3 6.4 copy-start.2
  180.3 4.3 copy-start.23
  190.1 423.9 %all-reduce.9.cloned.1.call-start = ((), (), s32[]{:S(2)}) async-start(), calls=%async_computation.1 | async-start | bytes 1048576 | tf_op jit(solution)/shard_map/psum | solution.py:171
  242.5 3.2 copy-start.19
  299.5 3.6 copy-start.35
  301.2 4.1 copy-start.18
  382.8 8.1 collective-permute-start.2
  386.6 19.3 %collective-permute-start = (bf16[256,512]{1,0:T(8,128)(2,1)}, bf16[256,512]{1,0:T(8,128)(2,1)}, u32[]{:S(2)}, u32[]{:S(2)}) collective-permute-start(bf16[256,512]{1,0:T(8,128)(2,1)} %fusion.93), channel_id=1, source_target_pairs={{0,16},{16,32},{32,48},{48,64},{64,80},{80,96},{96,112},{112,128},... | collective-permute-start | bytes 786440 | tf_op jit(solution)/shard_map/ppermute | solution.py:17
  390.9 3.4 copy-start.14
  400.6 3.5 copy-start.32
  405.8 6.0 copy-start.22
  416.2 3.9 copy-start.21
  420.0 426.0 %all-reduce.7.cloned.1.call-start = ((), (), s32[]{:S(2)}) async-start(), calls=%async_computation | async-start | bytes 1048576 | tf_op jit(solution)/shard_map/psum | solution.py:171
  614.0 10.9 %copy-start.4 = (bf16[256,768]{0,1:T(8,128)(2,1)S(1)}, bf16[256,768]{0,1:T(8,128)(2,1)}, u32[]{:S(2)}) copy-start(bf16[256,768]{0,1:T(8,128)(2,1)} %copy-done.3) | copy-start | bytes 1179652
  615.8 7.8 collective-permute-start.3
  619.5 18.5 %collective-permute-start.1 = (bf16[256,512]{1,0:T(8,128)(2,1)}, bf16[256,512]{1,0:T(8,128)(2,1)}, u32[]{:S(2)}, u32[]{:S(2)}) collective-permute-start(bf16[256,512]{1,0:T(8,128)(2,1)} %fusion.90), channel_id=1, source_target_pairs={{0,16},{16,32},{32,48},{48,64},{64,80},{80,96},{96,112},{112,128},... | collective-permute-start | bytes 786440 | tf_op jit(solution)/shard_map/ppermute | solution.py:17
  632.7 3.5 copy-start.29
  650.2 5.1 copy-start.30
  655.3 192.9 %copy-start.24 = (bf16[256,32]{0,1:T(8,128)(2,1)S(1)}, bf16[256,32]{0,1:T(8,128)(2,1)}, u32[]{:S(2)}) copy-start(bf16[256,32]{0,1:T(8,128)(2,1)} %copy.166) | copy-start | bytes 49156
  655.3 192.9 %copy-start.25 = (bf16[256,32]{0,1:T(8,128)(2,1)S(1)}, bf16[256,32]{0,1:T(8,128)(2,1)}, u32[]{:S(2)}) copy-start(bf16[256,32]{0,1:T(8,128)(2,1)} %copy.181) | copy-start | bytes 49156
  (26 other events, 41.4 us)
Sparse Core Ops, SparseCore 0:
  190.3 191.4 all-reduce.10
  420.1 193.8 all-reduce.8
  652.3 193.6 all-reduce.6
where the time goes:
time: 858 us; the launch traced here: 856 us
  waiting for transfers between devices  447 us (52%)
  blocking collectives  263 us (31%)
  matrix products  59.7 us (7%)
  other arithmetic  34.4 us (4%)
  local copies, waits for them, and re-layouts  28.4 us (3%)
  between operations  14.6 us (2%)
  starting transfers between devices  8.92 us (1%)
    psum x3, waiting for transfers between devices, body(): lax.psum(head_term.astype(jnp.bfloat16), 'tensor').astype(jnp.float32)  447 us
    all_gather x1, blocking collectives, body(): lax.all_gather(kept_inputs[0], 'tensor', axis=2, tiled=True)  65.1 us
    all_gather x1, blocking collectives, body(): lax.all_gather(objective_derivative_arrivals, 'tensor', axis=2, tiled=True)  51.2 us
    all_gather x1, blocking collectives, body(): lax.all_gather(encoded_arrivals, 'tensor', axis=2, tiled=True)  51.2 us
    all_gather x1, blocking collectives, body(): lax.all_gather(transit_latents[0], 'tensor', axis=1, tiled=True)  48.8 us
    all_gather x1, blocking collectives, body(): lax.all_gather(arriving_latent_derivative[0], 'tensor', axis=1, tiled=True)  46.8 us
    dot_general x21, matrix products, contract_heads(): return jnp.einsum(form, left, right, preferred_element_type=jnp.float32)  33.3 us
  transfers between devices with their start and end apart: 7, of which 3 were waited for; matrix products, arithmetic and copies ran while one was open for 7% of the time, Pallas kernels for 0%

commit v1 on v0

v1 whole, which is shorter than its diff:
```python
import functools

import jax
import jax.numpy as jnp
from jax import lax
from jax.experimental import pallas as pl
from jax.experimental.pallas import tpu as pltpu
from jax.sharding import PartitionSpec as P

HD = 128
SCALE = 8.0 / 128
NORM_EPS = 1e-05
HEAD_EPS = 1e-06
TICKS = 3
YS = 8
COPIES = 192
BF = jnp.bfloat16
F32 = jnp.float32


def mm(a, b):
    return jnp.dot(a, b, preferred_element_type=F32)


def mm_nt(a, b):
    return lax.dot_general(a, b, (((1,), (1,)), ((), ())), preferred_element_type=F32)


def kernel(
    sections,
    pieces_ref, flab_ref, blab_ref, w_ref, wo_ref,
    codes_ref, grads_ref, gq_ref, go_ref,
    full, part, rsb, zbuf, qsend, qown, qrecv,
    wt, wot, maskf, maskb,
    nt_s, q32_s, qn_s, kn_s, k32_s, v_s, p_s, pb_s, mix_s, fac_s, rr_s, dp_s,
    send_sems, recv_sems,
):
    feat, toks = 512, 256
    heads = w_ref.shape[1] // (3 * HD)
    s = lax.axis_index("section")
    rank = lax.axis_index("tensor")
    z = rank // YS
    y = rank % YS
    up, down = (y + 1) % YS, (y + YS - 1) % YS
    nxt, prv = (s + 1) % sections, (s + sections - 1) % sections

    def dev(sec, zz, yy):
        return {"section": sec, "tensor": zz * YS + yy}

    up_dev, down_dev, z_dev = dev(s, z, up), dev(s, z, down), dev(s, 1 - z, y)
    partners = (up_dev, down_dev, z_dev, dev(nxt, z, y), dev(nxt, 1 - z, y), dev(prv, z, y), dev(prv, 1 - z, y))
    barrier = pltpu.get_barrier_semaphore()
    for p in partners:
        pl.semaphore_signal(barrier, inc=1, device_id=p, device_id_type=pl.DeviceIdType.MESH)

    copies = []

    def send(src, dst, target):
        i = len(copies)
        c = pltpu.make_async_remote_copy(
            src_ref=src, dst_ref=dst, send_sem=send_sems.at[i], recv_sem=recv_sems.at[i],
            device_id=target, device_id_type=pl.DeviceIdType.MESH,
        )
        c.start()
        copies.append(c)
        return c

    def at(k):
        return (y + k + YS) % YS

    class Gather:
        def __init__(self, b):
            self.b = b

        def exchange(self, piece):
            full[self.b, z, y] = pieces_ref[piece]
            self.zc = send(full.at[self.b, z, y], full.at[self.b, z, y], z_dev)

        def start(self):
            ref = full.at[self.b, :, y]
            self.plus, self.minus = send(ref, ref, up_dev), send(ref, ref, down_dev)

        def step(self, k):
            self.plus.wait_recv()
            if k < 3:
                ref = full.at[self.b, :, at(-k)]
            else:
                ref = full.at[self.b, 0, at(-k)]
            self.plus = send(ref, ref, up_dev)
            self.minus.wait_recv()
            if k < 3:
                ref = full.at[self.b, :, at(k)]
            else:
                ref = full.at[self.b, 1, at(k)]
            self.minus = send(ref, ref, down_dev)

        def finish(self):
            self.plus.wait_recv()
            self.minus.wait_recv()

    class Reduce:
        def __init__(self, c, t):
            self.p = part.at[c, t]
            self.r = rsb.at[c, t]

        def start(self):
            self.plus = send(self.p.at[0, at(4)], self.r.at[0, 0, 0], up_dev)
            self.minus = send(self.p.at[1, at(-4)], self.r.at[1, 0, 1], down_dev)

        def step(self, k):
            p, r = self.p, self.r
            for d, copy, target, own in ((0, self.plus, up_dev, at(4 - k)), (1, self.minus, down_dev, at(k - 4))):
                copy.wait_recv()
                if k == 1:
                    r[d, 0, d] = r[d, 0, d] + p[d, own]
                    r[d, 0, 1 - d] = p[1 - d, own]
                else:
                    r[d, k - 1] = r[d, k - 1] + p[:, own]
                new = send(r.at[d, k - 1], r.at[d, k], target)
                if d == 0:
                    self.plus = new
                else:
                    self.minus = new

        def finish(self):
            self.plus.wait_recv()
            self.minus.wait_recv()
            return self.r[0, 3].astype(F32) + self.r[1, 3].astype(F32) + self.p[:, y].astype(F32)

    outs = []

    class Pass:
        def __init__(self, c, t):
            self.c, self.t = c, t

        def start(self, total, b):
            c, t = self.c, self.t
            zero = jnp.zeros((32, toks), F32)
            halves = []
            for h in range(2):
                halves.append((total[h] + jnp.where(z == h, full[b, h, y].astype(F32), zero)).astype(BF))
            qown[c, t, 0] = halves[0]
            qown[c, t, 1] = halves[1]
            outs.append((c, t, send(qown.at[c, t, 1 - z], qrecv.at[c, t], z_dev)))
            if t + 1 < TICKS:
                edge = (s == sections - 1) if c == 0 else (s == 0)
                entering = pieces_ref[(5 if c == 0 else 7) + t]
                none = jnp.zeros((32, toks), BF)
                for h in range(2):
                    own_half = jnp.where(z == h, entering, none)
                    qsend[c, t, h] = jnp.where(edge, own_half, halves[h])
                to = nxt if c == 0 else prv
                self.near = send(qsend.at[c, t], zbuf.at[c, t, 0], dev(to, z, y))
                self.far = send(qsend.at[c, t], zbuf.at[c, t, 1], dev(to, 1 - z, y))

        def arrive(self, b):
            self.near.wait_recv()
            self.far.wait_recv()
            c, t = self.c, self.t
            full[b, :, y] = (zbuf[c, t, 0].astype(F32) + zbuf[c, t, 1].astype(F32)).astype(BF)

    def slot(kind, t):
        return kind * TICKS + t

    def make_mask(ref, row, out, t):
        seg = jnp.broadcast_to(ref[pl.ds(row, 1), :].astype(F32), (toks, toks))
        segt = seg.T
        j = lax.broadcasted_iota(jnp.int32, (toks, toks), 0)
        i = lax.broadcasted_iota(jnp.int32, (toks, toks), 1)
        out[t] = jnp.where((j <= i) & (seg == segt), 1.0, 0.0)

    def normed(b):
        a = full[b].reshape(feat, toks).astype(F32)
        rr = lax.rsqrt(jnp.mean(a * a, axis=0, keepdims=True) + NORM_EPS)
        return a * rr, rr

    def head_norm(x):
        f = lax.rsqrt(jnp.mean(x * x, axis=0, keepdims=True) + HEAD_EPS)
        return x * f, f

    def probs(qn, kn, mask):
        w = jnp.exp(mm(kn, qn) * SCALE) * mask
        return w * (1.0 / jnp.sum(w, axis=0, keepdims=True))

    def forward(t):
        n32, _ = normed(slot(0, t))
        packed = mm(wt[...], n32.astype(BF)).astype(BF)
        mask = maskf[t]
        mixed = []
        for h in range(heads):
            base = 3 * HD * h
            q32, _ = head_norm(packed[base:base + HD].astype(F32))
            k32, _ = head_norm(packed[base + HD:base + 2 * HD].astype(F32))
            p = probs(q32.astype(BF), k32.astype(BF).T, mask)
            mixed.append(mm(packed[base + 2 * HD:base + 3 * HD], p.astype(BF)).astype(BF))
        term = mm(wot[...], jnp.concatenate(mixed, axis=0))
        part[0, t] = term.astype(BF).reshape(2, YS, 32, toks)

    def recompute(t):
        n32, rr = normed(slot(2, t))
        n = n32.astype(BF)
        nt_s[t] = n
        rr_s[t] = rr
        packed = mm(wt[...], n).astype(BF)
        mask = maskb[t]
        for h in range(heads):
            base = 3 * HD * h
            q32, sq = head_norm(packed[base:base + HD].astype(F32))
            k32, sk = head_norm(packed[base + HD:base + 2 * HD].astype(F32))
            v = packed[base + 2 * HD:base + 3 * HD]
            q32_s[t, h], k32_s[t, h] = q32, k32
            fac_s[t, h, 0:1], fac_s[t, h, 1:2] = sq, sk
            qn, kn = q32.astype(BF), k32.astype(BF)
            qn_s[t, h], kn_s[t, h] = qn, kn
            v_s[t, h] = v.T
            p = probs(qn, kn.T, mask)
            p_s[t, h] = p
            pb = p.astype(BF)
            pb_s[t, h] = pb
            mix_s[t, h * HD:(h + 1) * HD] = mm(v, pb).astype(BF)

    def norm_back(grad, unit, factor):
        return factor * (grad - unit * jnp.mean(grad * unit, axis=0, keepdims=True))

    def back_head(t, h):
        g = full[slot(1, t)].reshape(feat, toks)
        dm = mm(wo_ref[h * HD:(h + 1) * HD], g).astype(BF)
        dp = mm(v_s[t, h], dm)
        base = 3 * HD * h
        pb = pb_s[t, h]
        dp_s[t, base + 2 * HD:base + 3 * HD] = mm_nt(dm, pb).astype(BF)
        p = p_s[t, h]
        pd = p * dp
        inner = jnp.sum(pd, axis=0, keepdims=True)
        ds = ((pd - p * inner) * SCALE).astype(BF)
        dq = mm(kn_s[t, h], ds)
        dk = mm_nt(qn_s[t, h], ds)
        dp_s[t, base:base + HD] = norm_back(dq, q32_s[t, h], fac_s[t, h, 0:1]).astype(BF)
        dp_s[t, base + HD:base + 2 * HD] = norm_back(dk, k32_s[t, h], fac_s[t, h, 1:2]).astype(BF)

    def back_term(t):
        dn = mm(w_ref[...], dp_s[t])
        rr = rr_s[t]
        n32 = full[slot(2, t)].reshape(feat, toks).astype(F32) * rr
        part[1, t] = norm_back(dn, n32, rr).astype(BF).reshape(2, YS, 32, toks)

    def weight_terms(t):
        g = full[slot(1, t)].reshape(feat, toks)
        gq = mm_nt(nt_s[t], dp_s[t])
        go = mm_nt(mix_s[t], g)
        if t == 0:
            gq_ref[...] = gq
            go_ref[...] = go
        else:
            gq_ref[...] += gq
            go_ref[...] += go

    wt[...] = w_ref[...].T
    wot[...] = wo_ref[...].T
    pl.semaphore_wait(barrier, len(partners))

    ag_f = Gather(slot(0, 0))
    ag_g = Gather(slot(1, 0))
    ag_s = [Gather(slot(2, t)) for t in range(TICKS)]
    ag_f.exchange(0)
    ag_s[0].exchange(2)
    ag_g.exchange(1)
    ag_s[1].exchange(3)
    ag_s[2].exchange(4)
    for t in range(TICKS):
        make_mask(flab_ref, t - s + sections - 1, maskf, t)
        make_mask(blab_ref, t + s, maskb, t)
    ag_f.zc.wait_recv()
    ag_f.start()
    ag_s[0].zc.wait_recv()
    ag_s[0].start()
    ag_g.zc.wait_recv()
    ag_g.start()
    for k in (1, 2, 3):
        ag_f.step(k)
        ag_s[0].step(k)
        ag_g.step(k)
    ag_s[1].zc.wait_recv()
    ag_s[2].zc.wait_recv()
    ag_f.finish()

    for t in range(TICKS):
        more = t + 1 < TICKS
        forward(t)
        rs_f = Reduce(0, t)
        rs_f.start()
        if t == 0:
            ag_s[0].finish()
            ag_g.finish()
        else:
            pass_b.arrive(slot(1, t))
            ag_g = Gather(slot(1, t))
            ag_g.start()
        recompute(t)
        rs_f.step(1)
        if t > 0:
            ag_g.step(1)
            rs_f.step(2)
            ag_g.step(2)
            rs_f.step(3)
            ag_g.step(3)
            ag_g.finish()
        back_head(t, 0)
        if t == 0:
            rs_f.step(2)
        back_head(t, 1)
        if t == 0:
            rs_f.step(3)
        pass_f = Pass(0, t)
        if t > 0:
            pass_f.start(rs_f.finish(), slot(0, t))
        back_term(t)
        rs_b = Reduce(1, t)
        rs_b.start()
        if t == 0:
            pass_f.start(rs_f.finish(), slot(0, t))
        weight_terms(t)
        rs_b.step(1)
        if more:
            pass_f.arrive(slot(0, t + 1))
            ag_f = Gather(slot(0, t + 1))
            ag_f.start()
            ag_s[t + 1].start()
        rs_b.step(2)
        if more:
            ag_f.step(1)
            ag_s[t + 1].step(1)
        rs_b.step(3)
        if more:
            ag_f.step(2)
            ag_s[t + 1].step(2)
        pass_b = Pass(1, t)
        pass_b.start(rs_b.finish(), slot(1, t))
        if more:
            ag_f.step(3)
            ag_s[t + 1].step(3)
            ag_f.finish()
            ag_s[t + 1].finish()

    for c, t, copy in outs:
        copy.wait_recv()
        out = codes_ref if c == 0 else grads_ref
        out[t] = (qown[c, t, z].astype(F32) + qrecv[c, t].astype(F32)).astype(BF)
    for c in copies:
        c.wait_send()


def body(
    transit_latents,
    encoded_arrivals,
    arriving_latent_derivative,
    objective_derivative_arrivals,
    kept_inputs,
    onward_sequence_labels,
    reverse_sequence_labels,
    expander_attn_factors,
    outgoing_compressor_factors,
):
    sections = lax.axis_size("section")
    w, wo = expander_attn_factors[0], outgoing_compressor_factors[0]
    feat, cols = w.shape
    heads = cols // (3 * HD)
    toks = transit_latents.shape[1]
    pieces = jnp.concatenate(
        [transit_latents, arriving_latent_derivative, kept_inputs[0], encoded_arrivals, objective_derivative_arrivals],
        axis=0,
    ).swapaxes(1, 2)
    shard = pieces.shape[1]
    vm = pl.BlockSpec(memory_space=pltpu.VMEM)
    block = (2, YS, shard, toks)
    scratch = [
        pltpu.VMEM((3 * TICKS,) + block, BF),
        pltpu.VMEM((2, TICKS) + block, BF),
        pltpu.VMEM((2, TICKS, 2, 4, 2, shard, toks), BF),
        pltpu.VMEM((2, TICKS, 2, 2, shard, toks), BF),
        pltpu.VMEM((2, TICKS, 2, shard, toks), BF),
        pltpu.VMEM((2, TICKS, 2, shard, toks), BF),
        pltpu.VMEM((2, TICKS, shard, toks), BF),
        pltpu.VMEM((cols, feat), BF),
        pltpu.VMEM((feat, heads * HD), BF),
        pltpu.VMEM((TICKS, toks, toks), F32),
        pltpu.VMEM((TICKS, toks, toks), F32),
        pltpu.VMEM((TICKS, feat, toks), BF),
        pltpu.VMEM((TICKS, heads, HD, toks), F32),
        pltpu.VMEM((TICKS, heads, HD, toks), BF),
        pltpu.VMEM((TICKS, heads, HD, toks), BF),
        pltpu.VMEM((TICKS, heads, HD, toks), F32),
        pltpu.VMEM((TICKS, heads, toks, HD), BF),
        pltpu.VMEM((TICKS, heads, toks, toks), F32),
        pltpu.VMEM((TICKS, heads, toks, toks), BF),
        pltpu.VMEM((TICKS, heads * HD, toks), BF),
        pltpu.VMEM((TICKS, heads, 8, toks), F32),
        pltpu.VMEM((TICKS, 1, toks), F32),
        pltpu.VMEM((TICKS, cols, toks), BF),
        pltpu.SemaphoreType.DMA((COPIES,)),
        pltpu.SemaphoreType.DMA((COPIES,)),
    ]
    codes, grads, gq, go = pl.pallas_call(
        functools.partial(kernel, sections),
        out_shape=(
            jax.ShapeDtypeStruct((TICKS, shard, toks), BF),
            jax.ShapeDtypeStruct((TICKS, shard, toks), BF),
            jax.ShapeDtypeStruct(w.shape, F32),
            jax.ShapeDtypeStruct(wo.shape, F32),
        ),
        in_specs=[vm] * 5,
        out_specs=(vm, vm, vm, vm),
        scratch_shapes=scratch,
        compiler_params=pltpu.CompilerParams(
            collective_id=0, has_side_effects=True, vmem_limit_bytes=48 * 1024 * 1024
        ),
    )(pieces, onward_sequence_labels, reverse_sequence_labels, w, wo)
    return codes.swapaxes(1, 2)[None], grads.swapaxes(1, 2)[None], gq[None], go[None]


def solution(mesh):
    in_specs = (
        P("section", None, "tensor"),
        P(None, None, "tensor"),
        P("section", None, "tensor"),
        P(None, None, "tensor"),
        P("section", None, None, "tensor"),
        P(),
        P(),
        P("section", None, "tensor"),
        P("section", "tensor", None),
    )
    out_specs = (
        P("section", None, None, "tensor"),
        P("section", None, None, "tensor"),
        P("section", None, "tensor"),
        P("section", "tensor", None),
    )
    return jax.shard_map(body, mesh=mesh, in_specs=in_specs, out_specs=out_specs, check_vma=False)
```

time: 858 us -> 146 us (0.17)
  the two profiles are of different devices: /device:TPU:2 before, /device:TPU:8 now
where the time goes in v1:
time: 146 us; the launch traced here: 145 us
  Pallas kernels  134 us (92%)
  local copies, waits for them, and re-layouts  10.6 us (7%)
    pallas_call x1, Pallas kernels, body(): pl.pallas_call(functools.partial(kernel, sections), out_shape=(jax.ShapeD...  134 us
    unnamed x16, local copies, waits for them, and re-layouts  9.82 us

profile of v1, /device:TPU:8, one launch (start us, length us, event | category | flops | bytes accessed | tf_op | source)
XLA Modules:
  0.0 145.3 jit_solution(6277309196120671667)
XLA Ops:
  0.6 0.7 constant_dynamic-update-slice_fusion.3
  1.4 0.7 constant_dynamic-update-slice_fusion.2
  2.1 0.8 bitcast_dynamic-update-slice_fusion
  2.9 0.8 constant_dynamic-update-slice_fusion.1
  3.6 0.8 constant_dynamic-update-slice_fusion
  4.4 0.0 copy-start
  4.4 1.1 copy-done
  5.5 0.0 copy-start.1
  5.5 0.9 copy-done.1
  6.5 0.0 copy-start.2
  6.5 0.8 copy-done.2
  7.3 0.0 copy-start.3
  7.3 0.8 copy-done.3
  8.0 134.0 %shard_map.120 = (bf16[3,32,256]{2,1,0:T(8,128)(2,1)S(1)}, bf16[3,32,256]{2,1,0:T(8,128)(2,1)S(1)}, f32[512,768]{1,0:T(8,128)S(1)}, f32[256,512]{1,0:T(8,128)S(1)}) custom-call(bf16[9,32,256]{2,1,0:T(8,128)(2,1)S(1)} %bitcast.17, s32[34,256]{1,0:T(8,128)S(1)} %copy-done.2, s32[34,256]{1,0:T(8,128)S(1)} %copy-done.3, bf16[512,768]{1,0:T(8,128)(2,1)S(1)} %bitcast.14, ...), custom_call_target="tpu_custom_call" | custom-call | tf_op jit(solution)/shard_map/pallas_call | solution.py:403
  142.1 0.6 copy.21
  142.7 0.6 copy.22
  143.3 1.1 copy.23
  144.5 0.8 copy.24
Async XLA Ops:
  4.4 1.1 copy-start
  5.5 0.9 copy-start.1
  6.5 0.8 copy-start.2
  7.3 0.8 copy-start.3

commit v2 on v1

--- a/solution.py
+++ b/solution.py
@@ -28,12 +28,13 @@
 
 def kernel(
     sections,
-    pieces_ref, flab_ref, blab_ref, w_ref, wo_ref,
+    codes_hbm, feed_hbm, grad_hbm, loss_hbm, kept_hbm, flab_hbm, blab_hbm, w_hbm, wo_hbm,
     codes_ref, grads_ref, gq_ref, go_ref,
+    enter, flab_ref, blab_ref, w_ref, wo_ref,
     full, part, rsb, zbuf, qsend, qown, qrecv,
     wt, wot, maskf, maskb,
     nt_s, q32_s, qn_s, kn_s, k32_s, v_s, p_s, pb_s, mix_s, fac_s, rr_s, dp_s,
-    send_sems, recv_sems,
+    load_sems, send_sems, recv_sems,
 ):
     feat, toks = 512, 256
     heads = w_ref.shape[1] // (3 * HD)
@@ -41,17 +42,37 @@
     rank = lax.axis_index("tensor")
     z = rank // YS
     y = rank % YS
-    up, down = (y + 1) % YS, (y + YS - 1) % YS
+
+    def at(k):
+        return (y + k + YS) % YS
+
     nxt, prv = (s + 1) % sections, (s + sections - 1) % sections
 
     def dev(sec, zz, yy):
         return {"section": sec, "tensor": zz * YS + yy}
 
-    up_dev, down_dev, z_dev = dev(s, z, up), dev(s, z, down), dev(s, 1 - z, y)
-    partners = (up_dev, down_dev, z_dev, dev(nxt, z, y), dev(nxt, 1 - z, y), dev(prv, z, y), dev(prv, 1 - z, y))
+    ring = {k: dev(s, z, at(k)) for k in (1, -1, 2, -2)}
+    z_dev = dev(s, 1 - z, y)
+    partners = (*ring.values(), z_dev, dev(nxt, z, y), dev(nxt, 1 - z, y), dev(prv, z, y), dev(prv, 1 - z, y))
     barrier = pltpu.get_barrier_semaphore()
     for p in partners:
         pl.semaphore_signal(barrier, inc=1, device_id=p, device_id_type=pl.DeviceIdType.MESH)
+
+    loads = []
+    for src, dst in (
+        (kept_hbm.at[0], full.at[pl.ds(2 * TICKS, TICKS), z, y]),
+        (grad_hbm, full.at[pl.ds(TICKS, 1), z, y]),
+        (codes_hbm, full.at[pl.ds(0, 1), z, y]),
+        (w_hbm.at[0], w_ref),
+        (wo_hbm.at[0], wo_ref),
+        (blab_hbm, blab_ref),
+        (flab_hbm, flab_ref),
+        (feed_hbm, enter.at[0]),
+        (loss_hbm, enter.at[1]),
+    ):
+        load = pltpu.make_async_copy(src, dst, load_sems.at[len(loads)])
+        load.start()
+        loads.append(load)
 
     copies = []
 
@@ -65,38 +86,31 @@
         copies.append(c)
         return c
 
-    def at(k):
-        return (y + k + YS) % YS
-
     class Gather:
-        def __init__(self, b):
-            self.b = b
-
-        def exchange(self, piece):
-            full[self.b, z, y] = pieces_ref[piece]
-            self.zc = send(full.at[self.b, z, y], full.at[self.b, z, y], z_dev)
+        def __init__(self, b, half=None):
+            if half is None:
+                self.block = lambda k: full.at[b, :, at(k)]
+                self.parts = lambda k, h: full.at[b, h, at(k)]
+            else:
+                self.block = lambda k: full.at[b, half, at(k)]
+                self.parts = lambda k, h: full.at[b, half, at(k), pl.ds(16 * h, 16)]
 
         def start(self):
-            ref = full.at[self.b, :, y]
-            self.plus, self.minus = send(ref, ref, up_dev), send(ref, ref, down_dev)
-
-        def step(self, k):
-            self.plus.wait_recv()
-            if k < 3:
-                ref = full.at[self.b, :, at(-k)]
-            else:
-                ref = full.at[self.b, 0, at(-k)]
-            self.plus = send(ref, ref, up_dev)
-            self.minus.wait_recv()
-            if k < 3:
-                ref = full.at[self.b, :, at(k)]
-            else:
-                ref = full.at[self.b, 1, at(k)]
-            self.minus = send(ref, ref, down_dev)
+            own = self.block(0)
+            self.two = [send(own, own, ring[2]), send(own, own, ring[-2])]
+            self.rest = [send(own, own, ring[1]), send(own, own, ring[-1])]
+
+        def mid(self):
+            for i, d in enumerate((1, -1)):
+                self.two[i].wait_recv()
+                far = self.parts(-2 * d, i)
+                self.rest.append(send(far, far, ring[2 * d]))
+                block = self.block(-2 * d)
+                self.rest.append(send(block, block, ring[d]))
 
         def finish(self):
-            self.plus.wait_recv()
-            self.minus.wait_recv()
+            for c in self.rest:
+                c.wait_recv()
 
     class Reduce:
         def __init__(self, c, t):
@@ -104,28 +118,32 @@
             self.r = rsb.at[c, t]
 
         def start(self):
-            self.plus = send(self.p.at[0, at(4)], self.r.at[0, 0, 0], up_dev)
-            self.minus = send(self.p.at[1, at(-4)], self.r.at[1, 0, 1], down_dev)
-
-        def step(self, k):
             p, r = self.p, self.r
-            for d, copy, target, own in ((0, self.plus, up_dev, at(4 - k)), (1, self.minus, down_dev, at(k - 4))):
-                copy.wait_recv()
-                if k == 1:
-                    r[d, 0, d] = r[d, 0, d] + p[d, own]
-                    r[d, 0, 1 - d] = p[1 - d, own]
-                else:
-                    r[d, k - 1] = r[d, k - 1] + p[:, own]
-                new = send(r.at[d, k - 1], r.at[d, k], target)
-                if d == 0:
-                    self.plus = new
-                else:
-                    self.minus = new
+            self.first = []
+            for i, d in enumerate((1, -1)):
+                far = send(p.at[i, at(4 * d)], r.at[i, 1, i], ring[2 * d])
+                self.first.append((far, send(p.at[:, at(3 * d)], r.at[i, 0], ring[d])))
+            self.rest = [send(p.at[:, at(d)], r.at[i, 3], ring[d]) for i, d in enumerate((1, -1))]
+
+        def mid(self):
+            p, r = self.p, self.r
+            for i, d in enumerate((1, -1)):
+                for c in self.first[i]:
+                    c.wait_recv()
+                own = at(2 * d)
+                both = r[i, 0, i].astype(F32) + r[i, 1, i].astype(F32) + p[i, own].astype(F32)
+                r[i, 0, i] = both.astype(BF)
+                r[i, 0, 1 - i] = r[i, 0, 1 - i] + p[1 - i, own]
+                self.rest.append(send(r.at[i, 0], r.at[i, 2], ring[2 * d]))
 
         def finish(self):
-            self.plus.wait_recv()
-            self.minus.wait_recv()
-            return self.r[0, 3].astype(F32) + self.r[1, 3].astype(F32) + self.p[:, y].astype(F32)
+            for c in self.rest:
+                c.wait_recv()
+            r = self.r
+            total = self.p[:, y].astype(F32)
+            for i in range(2):
+                total = total + r[i, 2].astype(F32) + r[i, 3].astype(F32)
+            return total
 
     outs = []
 
@@ -141,17 +159,17 @@
                 halves.append((total[h] + jnp.where(z == h, full[b, h, y].astype(F32), zero)).astype(BF))
             qown[c, t, 0] = halves[0]
             qown[c, t, 1] = halves[1]
-            outs.append((c, t, send(qown.at[c, t, 1 - z], qrecv.at[c, t], z_dev)))
             if t + 1 < TICKS:
                 edge = (s == sections - 1) if c == 0 else (s == 0)
-                entering = pieces_ref[(5 if c == 0 else 7) + t]
+                entering = enter[c, t]
                 none = jnp.zeros((32, toks), BF)
                 for h in range(2):
                     own_half = jnp.where(z == h, entering, none)
                     qsend[c, t, h] = jnp.where(edge, own_half, halves[h])
                 to = nxt if c == 0 else prv
+                self.far = send(qsend.at[c, t], zbuf.at[c, t, 1], dev(to, 1 - z, y))
                 self.near = send(qsend.at[c, t], zbuf.at[c, t, 0], dev(to, z, y))
-                self.far = send(qsend.at[c, t], zbuf.at[c, t, 1], dev(to, 1 - z, y))
+            outs.append((c, t, send(qown.at[c, t, 1 - z], qrecv.at[c, t], z_dev)))
 
         def arrive(self, b):
             self.near.wait_recv()
@@ -255,92 +273,85 @@
             gq_ref[...] += gq
             go_ref[...] += go
 
+    def backward(t):
+        for h in range(heads):
+            back_head(t, h)
+        back_term(t)
+
+    for load in loads[:3]:
+        load.wait()
+    pl.semaphore_wait(barrier, len(partners))
+
+    order = [slot(2, 0), slot(1, 0), slot(0, 0)]
+    across = {}
+    for b in order + [slot(2, 1), slot(2, 2)]:
+        across[b] = send(full.at[b, z, y], full.at[b, z, y], z_dev)
+    mine = [Gather(b, z) for b in order]
+    others = [Gather(b, 1 - z) for b in order]
+    for g in mine:
+        g.start()
+    for load in loads[3:]:
+        load.wait()
     wt[...] = w_ref[...].T
     wot[...] = wo_ref[...].T
-    pl.semaphore_wait(barrier, len(partners))
-
-    ag_f = Gather(slot(0, 0))
-    ag_g = Gather(slot(1, 0))
-    ag_s = [Gather(slot(2, t)) for t in range(TICKS)]
-    ag_f.exchange(0)
-    ag_s[0].exchange(2)
-    ag_g.exchange(1)
-    ag_s[1].exchange(3)
-    ag_s[2].exchange(4)
+    for g in mine:
+        g.mid()
+    make_mask(blab_ref, s, maskb, 0)
+    make_mask(flab_ref, sections - 1 - s, maskf, 0)
+    for b, g in zip(order, others):
+        across[b].wait_recv()
+        g.start()
+    for t in range(1, TICKS):
+        make_mask(blab_ref, t + s, maskb, t)
+        make_mask(flab_ref, t - s + sections - 1, maskf, t)
+    for g in mine:
+        g.finish()
+    for g in others:
+        g.mid()
+    others[0].finish()
+    recompute(0)
+    others[1].finish()
+
+    reduce_b, reduce_f, pass_b, pass_f, kept = {}, {}, {}, {}, {}
     for t in range(TICKS):
-        make_mask(flab_ref, t - s + sections - 1, maskf, t)
-        make_mask(blab_ref, t + s, maskb, t)
-    ag_f.zc.wait_recv()
-    ag_f.start()
-    ag_s[0].zc.wait_recv()
-    ag_s[0].start()
-    ag_g.zc.wait_recv()
-    ag_g.start()
-    for k in (1, 2, 3):
-        ag_f.step(k)
-        ag_s[0].step(k)
-        ag_g.step(k)
-    ag_s[1].zc.wait_recv()
-    ag_s[2].zc.wait_recv()
-    ag_f.finish()
-
-    for t in range(TICKS):
-        more = t + 1 < TICKS
+        last = t + 1 == TICKS
+        if t > 0:
+            gather_b.finish()
+            recompute(t)
+        backward(t)
+        reduce_b[t] = Reduce(1, t)
+        reduce_b[t].start()
+        if t == 0:
+            others[2].finish()
+        else:
+            gather_f.mid()
+        weight_terms(t)
+        reduce_b[t].mid()
+        if t > 0:
+            gather_f.finish()
         forward(t)
-        rs_f = Reduce(0, t)
-        rs_f.start()
-        if t == 0:
-            ag_s[0].finish()
-            ag_g.finish()
-        else:
-            pass_b.arrive(slot(1, t))
-            ag_g = Gather(slot(1, t))
-            ag_g.start()
-        recompute(t)
-        rs_f.step(1)
-        if t > 0:
-            ag_g.step(1)
-            rs_f.step(2)
-            ag_g.step(2)
-            rs_f.step(3)
-            ag_g.step(3)
-            ag_g.finish()
-        back_head(t, 0)
-        if t == 0:
-            rs_f.step(2)
-        back_head(t, 1)
-        if t == 0:
-            rs_f.step(3)
-        pass_f = Pass(0, t)
-        if t > 0:
-            pass_f.start(rs_f.finish(), slot(0, t))
-        back_term(t)
-        rs_b = Reduce(1, t)
-        rs_b.start()
-        if t == 0:
-            pass_f.start(rs_f.finish(), slot(0, t))
-        weight_terms(t)
-        rs_b.step(1)
-        if more:
-            pass_f.arrive(slot(0, t + 1))
-            ag_f = Gather(slot(0, t + 1))
-            ag_f.start()
-            ag_s[t + 1].start()
-        rs_b.step(2)
-        if more:
-            ag_f.step(1)
-            ag_s[t + 1].step(1)
-        rs_b.step(3)
-        if more:
-            ag_f.step(2)
-            ag_s[t + 1].step(2)
-        pass_b = Pass(1, t)
-        pass_b.start(rs_b.finish(), slot(1, t))
-        if more:
-            ag_f.step(3)
-            ag_s[t + 1].step(3)
-            ag_f.finish()
-            ag_s[t + 1].finish()
+        reduce_f[t] = Reduce(0, t)
+        reduce_f[t].start()
+        pass_b[t] = Pass(1, t)
+        pass_b[t].start(reduce_b[t].finish(), slot(1, t))
+        if not last:
+            across[slot(2, t + 1)].wait_recv()
+            kept = Gather(slot(2, t + 1))
+            kept.start()
+        reduce_f[t].mid()
+        if not last:
+            pass_b[t].arrive(slot(1, t + 1))
+            gather_b = Gather(slot(1, t + 1))
+            gather_b.start()
+            kept.mid()
+        pass_f[t] = Pass(0, t)
+        pass_f[t].start(reduce_f[t].finish(), slot(0, t))
+        if not last:
+            gather_b.mid()
+            pass_f[t].arrive(slot(0, t + 1))
+            gather_f = Gather(slot(0, t + 1))
+            gather_f.start()
+            kept.finish()
 
     for c, t, copy in outs:
         copy.wait_recv()
@@ -362,18 +373,19 @@
     outgoing_compressor_factors,
 ):
     sections = lax.axis_size("section")
-    w, wo = expander_attn_factors[0], outgoing_compressor_factors[0]
+    w, wo = jax.ShapeDtypeStruct(expander_attn_factors.shape[1:], BF), jax.ShapeDtypeStruct(outgoing_compressor_factors.shape[1:], BF)
     feat, cols = w.shape
     heads = cols // (3 * HD)
-    toks = transit_latents.shape[1]
-    pieces = jnp.concatenate(
-        [transit_latents, arriving_latent_derivative, kept_inputs[0], encoded_arrivals, objective_derivative_arrivals],
-        axis=0,
-    ).swapaxes(1, 2)
-    shard = pieces.shape[1]
+    toks, shard = transit_latents.shape[1:]
     vm = pl.BlockSpec(memory_space=pltpu.VMEM)
     block = (2, YS, shard, toks)
+    hbm = pl.BlockSpec(memory_space=pl.ANY)
     scratch = [
+        pltpu.VMEM((2, TICKS - 1, shard, toks), BF),
+        pltpu.VMEM(onward_sequence_labels.shape, jnp.int32),
+        pltpu.VMEM(reverse_sequence_labels.shape, jnp.int32),
+        pltpu.VMEM((feat, cols), BF),
+        pltpu.VMEM((heads * HD, feat), BF),
         pltpu.VMEM((3 * TICKS,) + block, BF),
         pltpu.VMEM((2, TICKS) + block, BF),
         pltpu.VMEM((2, TICKS, 2, 4, 2, shard, toks), BF),
@@ -397,6 +409,7 @@
         pltpu.VMEM((TICKS, heads, 8, toks), F32),
         pltpu.VMEM((TICKS, 1, toks), F32),
         pltpu.VMEM((TICKS, cols, toks), BF),
+        pltpu.SemaphoreType.DMA((9,)),
         pltpu.SemaphoreType.DMA((COPIES,)),
         pltpu.SemaphoreType.DMA((COPIES,)),
     ]
@@ -408,13 +421,23 @@
             jax.ShapeDtypeStruct(w.shape, F32),
             jax.ShapeDtypeStruct(wo.shape, F32),
         ),
-        in_specs=[vm] * 5,
+        in_specs=[hbm] * 9,
         out_specs=(vm, vm, vm, vm),
         scratch_shapes=scratch,
         compiler_params=pltpu.CompilerParams(
-            collective_id=0, has_side_effects=True, vmem_limit_bytes=48 * 1024 * 1024
+            collective_id=0, has_side_effects=True, vmem_limit_bytes=60 * 1024 * 1024
         ),
-    )(pieces, onward_sequence_labels, reverse_sequence_labels, w, wo)
+    )(
+        transit_latents.swapaxes(1, 2),
+        encoded_arrivals.swapaxes(1, 2),
+        arriving_latent_derivative.swapaxes(1, 2),
+        objective_derivative_arrivals.swapaxes(1, 2),
+        kept_inputs.swapaxes(2, 3),
+        onward_sequence_labels,
+        reverse_sequence_labels,
+        expander_attn_factors,
+        outgoing_compressor_factors,
+    )
     return codes.swapaxes(1, 2)[None], grads.swapaxes(1, 2)[None], gq[None], go[None]
 
 

time: 146 us -> 109 us (0.75)
  the two profiles are of different devices: /device:TPU:8 before, /device:TPU:2 now
where the time goes in v2:
time: 109 us
  Pallas kernels  102 us (94%)
  local copies, waits for them, and re-layouts  6.35 us (6%)
    pallas_call x1, Pallas kernels, body(): pl.pallas_call(functools.partial(kernel, sections), out_shape=(jax.ShapeD...  102 us
    unnamed x6, local copies, waits for them, and re-layouts  6.35 us

profile of v2, /device:TPU:2, one launch (start us, length us, event | category | flops | bytes accessed | tf_op | source)
XLA Modules:
  0.0 108.5 jit_solution(10701976296644642325)
XLA Ops:
  0.6 101.6 %shard_map.120 = (bf16[3,32,256]{2,1,0:T(8,128)(2,1)}, bf16[3,32,256]{2,1,0:T(8,128)(2,1)}, f32[512,768]{1,0:T(8,128)}, f32[256,512]{1,0:T(8,128)}) custom-call(bf16[1,32,256]{2,1,0:T(8,128)(2,1)} %bitcast.20, bf16[2,32,256]{2,1,0:T(8,128)(2,1)} %bitcast.18, bf16[1,32,256]{2,1,0:T(8,128)(2,1)} %bitcast.21, bf16[2,32,256]{2,1,0:T(8,128)(2,1)} %bitcast.19, ...), custom_call_target="tpu_custom_call" | custom-call | tf_op jit(solution)/shard_map/pallas_call | solution.py:416
  102.2 1.4 %copy.17 = bf16[1,3,256,32]{2,3,1,0:T(8,128)(2,1)} copy(bf16[1,3,256,32]{2,3,1,0:T(8,128)(2,1)} %bitcast.17) | data formatting | bytes 98304
  103.6 1.4 %copy.18 = bf16[1,3,256,32]{2,3,1,0:T(8,128)(2,1)} copy(bf16[1,3,256,32]{2,3,1,0:T(8,128)(2,1)} %bitcast.16) | data formatting | bytes 98304
  105.0 0.0 copy-start
  105.0 2.7 %copy.19 = f32[1,512,768]{2,1,0:T(8,128)} copy(f32[1,512,768]{2,1,0:T(8,128)} %bitcast.13) | data formatting | bytes 3145728
  107.8 0.0 copy-done
  107.8 0.8 copy.20
Async XLA Ops:
  105.0 2.7 %copy-start = (f32[256,512]{1,0:T(8,128)S(1)}, f32[256,512]{1,0:T(8,128)}, u32[]{:S(2)}) copy-start(f32[256,512]{1,0:T(8,128)} %get-tuple-element.11) | copy-start | bytes 1572868

commit v3 on v2

--- a/solution.py
+++ b/solution.py
@@ -13,7 +13,7 @@
 HEAD_EPS = 1e-06
 TICKS = 3
 YS = 8
-COPIES = 192
+COPIES = 352
 BF = jnp.bfloat16
 F32 = jnp.float32
 
@@ -29,7 +29,7 @@
 def kernel(
     sections,
     codes_hbm, feed_hbm, grad_hbm, loss_hbm, kept_hbm, flab_hbm, blab_hbm, w_hbm, wo_hbm,
-    codes_ref, grads_ref, gq_ref, go_ref,
+    out_ref, gq_ref, go_ref,
     enter, flab_ref, blab_ref, w_ref, wo_ref,
     full, part, rsb, zbuf, qsend, qown, qrecv,
     wt, wot, maskf, maskb,
@@ -87,13 +87,9 @@
         return c
 
     class Gather:
-        def __init__(self, b, half=None):
-            if half is None:
-                self.block = lambda k: full.at[b, :, at(k)]
-                self.parts = lambda k, h: full.at[b, h, at(k)]
-            else:
-                self.block = lambda k: full.at[b, half, at(k)]
-                self.parts = lambda k, h: full.at[b, half, at(k), pl.ds(16 * h, 16)]
+        def __init__(self, b, h):
+            self.block = lambda k: full.at[b, h, at(k)]
+            self.parts = lambda k, i: full.at[b, h, at(k), pl.ds(16 * i, 16)]
 
         def start(self):
             own = self.block(0)
@@ -113,34 +109,37 @@
                 c.wait_recv()
 
     class Reduce:
-        def __init__(self, c, t):
-            self.p = part.at[c, t]
-            self.r = rsb.at[c, t]
+        def __init__(self, c, t, h):
+            self.h = h
+            self.p = part.at[c, t, h]
+            self.r = rsb.at[c, t, h]
 
         def start(self):
             p, r = self.p, self.r
             self.first = []
             for i, d in enumerate((1, -1)):
-                far = send(p.at[i, at(4 * d)], r.at[i, 1, i], ring[2 * d])
-                self.first.append((far, send(p.at[:, at(3 * d)], r.at[i, 0], ring[d])))
-            self.rest = [send(p.at[:, at(d)], r.at[i, 3], ring[d]) for i, d in enumerate((1, -1))]
+                rows = pl.ds(16 * i, 16)
+                far = send(p.at[at(4 * d), rows], r.at[i, 1, rows], ring[2 * d])
+                self.first.append((far, send(p.at[at(3 * d)], r.at[i, 0], ring[d])))
+            self.rest = [send(p.at[at(d)], r.at[i, 3], ring[d]) for i, d in enumerate((1, -1))]
 
         def mid(self):
             p, r = self.p, self.r
             for i, d in enumerate((1, -1)):
                 for c in self.first[i]:
                     c.wait_recv()
-                own = at(2 * d)
-                both = r[i, 0, i].astype(F32) + r[i, 1, i].astype(F32) + p[i, own].astype(F32)
-                r[i, 0, i] = both.astype(BF)
-                r[i, 0, 1 - i] = r[i, 0, 1 - i] + p[1 - i, own]
+                both = r[i, 0].astype(F32) + p[at(2 * d)].astype(F32)
+                far = r[i, 1, 16 * i:16 * i + 16].astype(F32)
+                none = jnp.zeros_like(far)
+                both = both + jnp.concatenate([far, none] if i == 0 else [none, far], axis=0)
+                r[i, 0] = both.astype(BF)
                 self.rest.append(send(r.at[i, 0], r.at[i, 2], ring[2 * d]))
 
         def finish(self):
             for c in self.rest:
                 c.wait_recv()
             r = self.r
-            total = self.p[:, y].astype(F32)
+            total = self.p[y].astype(F32)
             for i in range(2):
                 total = total + r[i, 2].astype(F32) + r[i, 3].astype(F32)
             return total
@@ -148,34 +147,63 @@
     outs = []
 
     class Pass:
-        def __init__(self, c, t):
-            self.c, self.t = c, t
+        def __init__(self, c, t, h):
+            self.c, self.t, self.h = c, t, h
 
         def start(self, total, b):
-            c, t = self.c, self.t
-            zero = jnp.zeros((32, toks), F32)
-            halves = []
-            for h in range(2):
-                halves.append((total[h] + jnp.where(z == h, full[b, h, y].astype(F32), zero)).astype(BF))
-            qown[c, t, 0] = halves[0]
-            qown[c, t, 1] = halves[1]
+            c, t, h = self.c, self.t, self.h
+            none = jnp.zeros((32, toks), F32)
+            rows = (total + jnp.where(z == h, full[b, h, y].astype(F32), none)).astype(BF)
+            qown[c, t, h] = rows
             if t + 1 < TICKS:
                 edge = (s == sections - 1) if c == 0 else (s == 0)
-                entering = enter[c, t]
-                none = jnp.zeros((32, toks), BF)
-                for h in range(2):
-                    own_half = jnp.where(z == h, entering, none)
-                    qsend[c, t, h] = jnp.where(edge, own_half, halves[h])
+                entering = jnp.where(z == h, enter[c, t], none.astype(BF))
+                qsend[c, t, h] = jnp.where(edge, entering, rows)
                 to = nxt if c == 0 else prv
-                self.far = send(qsend.at[c, t], zbuf.at[c, t, 1], dev(to, 1 - z, y))
-                self.near = send(qsend.at[c, t], zbuf.at[c, t, 0], dev(to, z, y))
-            outs.append((c, t, send(qown.at[c, t, 1 - z], qrecv.at[c, t], z_dev)))
+                self.far = send(qsend.at[c, t, h], zbuf.at[c, t, 1, h], dev(to, 1 - z, y))
+                self.near = send(qsend.at[c, t, h], zbuf.at[c, t, 0, h], dev(to, z, y))
 
         def arrive(self, b):
             self.near.wait_recv()
             self.far.wait_recv()
+            c, t, h = self.c, self.t, self.h
+            full[b, h, y] = (zbuf[c, t, 0, h].astype(F32) + zbuf[c, t, 1, h].astype(F32)).astype(BF)
+
+    class Chain:
+        def __init__(self, c, t):
+            self.c, self.t = c, t
+            self.halves = (0, 1) if t + 1 < TICKS else (1 - z, z)
+            self.reduces = [Reduce(c, t, h) for h in self.halves]
+            self.passes = [Pass(c, t, h) for h in self.halves]
+            self.gathers = [Gather(slot(c, t + 1), h) for h in self.halves]
+
+        def reduce_start(self):
+            for r in self.reduces:
+                r.start()
+
+        def reduce_mid(self):
+            for r in self.reduces:
+                r.mid()
+
+        def hand_over(self):
             c, t = self.c, self.t
-            full[b, :, y] = (zbuf[c, t, 0].astype(F32) + zbuf[c, t, 1].astype(F32)).astype(BF)
+            for i in range(2):
+                self.passes[i].start(self.reduces[i].finish(), slot(c, t))
+                if i == (0 if t + 1 == TICKS else 1):
+                    outs.append((c, t, send(qown.at[c, t, 1 - z], qrecv.at[c, t], z_dev)))
+
+        def gather_start(self):
+            for i in range(2):
+                self.passes[i].arrive(slot(self.c, self.t + 1))
+                self.gathers[i].start()
+
+        def gather_mid(self):
+            for g in self.gathers:
+                g.mid()
+
+        def gather_finish(self):
+            for g in self.gathers:
+                g.finish()
 
     def slot(kind, t):
         return kind * TICKS + t
@@ -312,53 +340,61 @@
     recompute(0)
     others[1].finish()
 
-    reduce_b, reduce_f, pass_b, pass_f, kept = {}, {}, {}, {}, {}
     for t in range(TICKS):
         last = t + 1 == TICKS
         if t > 0:
-            gather_b.finish()
-            recompute(t)
+            old_f, old_b = chain_f, chain_b
+            old_b.gather_finish()
         backward(t)
-        reduce_b[t] = Reduce(1, t)
-        reduce_b[t].start()
+        chain_f, chain_b = Chain(0, t), Chain(1, t)
+        chain_b.reduce_start()
         if t == 0:
             others[2].finish()
         else:
-            gather_f.mid()
+            old_f.gather_finish()
+        forward(t)
+        chain_f.reduce_start()
         weight_terms(t)
-        reduce_b[t].mid()
-        if t > 0:
-            gather_f.finish()
-        forward(t)
-        reduce_f[t] = Reduce(0, t)
-        reduce_f[t].start()
-        pass_b[t] = Pass(1, t)
-        pass_b[t].start(reduce_b[t].finish(), slot(1, t))
+        chain_b.reduce_mid()
+        chain_f.reduce_mid()
+        chain_b.hand_over()
+        chain_f.hand_over()
         if not last:
             across[slot(2, t + 1)].wait_recv()
-            kept = Gather(slot(2, t + 1))
-            kept.start()
-        reduce_f[t].mid()
-        if not last:
-            pass_b[t].arrive(slot(1, t + 1))
-            gather_b = Gather(slot(1, t + 1))
-            gather_b.start()
-            kept.mid()
-        pass_f[t] = Pass(0, t)
-        pass_f[t].start(reduce_f[t].finish(), slot(0, t))
-        if not last:
-            gather_b.mid()
-            pass_f[t].arrive(slot(0, t + 1))
-            gather_f = Gather(slot(0, t + 1))
-            gather_f.start()
-            kept.finish()
+            kept = [Gather(slot(2, t + 1), h) for h in range(2)]
+            for g in kept:
+                g.start()
+            chain_b.gather_start()
+            chain_f.gather_start()
+            for g in kept:
+                g.mid()
+            chain_b.gather_mid()
+            chain_f.gather_mid()
+            for g in kept:
+                g.finish()
+            recompute(t + 1)
 
     for c, t, copy in outs:
         copy.wait_recv()
-        out = codes_ref if c == 0 else grads_ref
-        out[t] = (qown[c, t, z].astype(F32) + qrecv[c, t].astype(F32)).astype(BF)
+        out_ref[c, t] = (qown[c, t, z].astype(F32) + qrecv[c, t].astype(F32)).astype(BF)
     for c in copies:
         c.wait_send()
+
+
+def hand_out(out_ref, gq_ref, go_ref, codes, grads, gq, go, out_v, gq_v, go_v, sems):
+    rows = gq.shape[0] // 4
+    moves = [(gq_ref.at[part], gq_v.at[part], gq.at[part]) for part in (pl.ds(rows * i, rows) for i in range(4))]
+    moves.append((go_ref, go_v, go))
+    moves += [(out_ref.at[i], out_v.at[i], out) for i, out in enumerate((codes, grads))]
+    loads = [pltpu.make_async_copy(a, b, sems.at[0, i]) for i, (a, b, _) in enumerate(moves)]
+    stores = [pltpu.make_async_copy(b, c, sems.at[1, i]) for i, (_, b, c) in enumerate(moves)]
+    for c in loads:
+        c.start()
+    for load, store in zip(loads, stores):
+        load.wait()
+        store.start()
+    for c in stores:
+        c.wait()
 
 
 def body(
@@ -388,7 +424,7 @@
         pltpu.VMEM((heads * HD, feat), BF),
         pltpu.VMEM((3 * TICKS,) + block, BF),
         pltpu.VMEM((2, TICKS) + block, BF),
-        pltpu.VMEM((2, TICKS, 2, 4, 2, shard, toks), BF),
+        pltpu.VMEM((2, TICKS, 2, 2, 4, shard, toks), BF),
         pltpu.VMEM((2, TICKS, 2, 2, shard, toks), BF),
         pltpu.VMEM((2, TICKS, 2, shard, toks), BF),
         pltpu.VMEM((2, TICKS, 2, shard, toks), BF),
@@ -413,16 +449,15 @@
         pltpu.SemaphoreType.DMA((COPIES,)),
         pltpu.SemaphoreType.DMA((COPIES,)),
     ]
-    codes, grads, gq, go = pl.pallas_call(
+    out, gq, go = pl.pallas_call(
         functools.partial(kernel, sections),
         out_shape=(
-            jax.ShapeDtypeStruct((TICKS, shard, toks), BF),
-            jax.ShapeDtypeStruct((TICKS, shard, toks), BF),
+            jax.ShapeDtypeStruct((2, TICKS, shard, toks), BF),
             jax.ShapeDtypeStruct(w.shape, F32),
             jax.ShapeDtypeStruct(wo.shape, F32),
         ),
         in_specs=[hbm] * 9,
-        out_specs=(vm, vm, vm, vm),
+        out_specs=(vm, vm, vm),
         scratch_shapes=scratch,
         compiler_params=pltpu.CompilerParams(
             collective_id=0, has_side_effects=True, vmem_limit_bytes=60 * 1024 * 1024
@@ -438,6 +473,24 @@
         expander_attn_factors,
         outgoing_compressor_factors,
     )
+    codes, grads, gq, go = pl.pallas_call(
+        hand_out,
+        out_shape=(
+            jax.ShapeDtypeStruct(out.shape[1:], BF),
+            jax.ShapeDtypeStruct(out.shape[1:], BF),
+            jax.ShapeDtypeStruct(gq.shape, F32),
+            jax.ShapeDtypeStruct(go.shape, F32),
+        ),
+        in_specs=[hbm] * 3,
+        out_specs=[hbm] * 4,
+        scratch_shapes=[
+            pltpu.VMEM(out.shape, BF),
+            pltpu.VMEM(gq.shape, F32),
+            pltpu.VMEM(go.shape, F32),
+            pltpu.SemaphoreType.DMA((2, 7)),
+        ],
+        compiler_params=pltpu.CompilerParams(vmem_limit_bytes=60 * 1024 * 1024),
+    )(out, gq, go)
     return codes.swapaxes(1, 2)[None], grads.swapaxes(1, 2)[None], gq[None], go[None]
 
 

time: 109 us -> 103 us (0.945)
  the two profiles are of different devices: /device:TPU:2 before, /device:TPU:8 now
where the time goes in v3:
time: 103 us
  Pallas kernels  103 us (100%)
    pallas_call x1, Pallas kernels, body(): pl.pallas_call(functools.partial(kernel, sections), out_shape=(jax.ShapeD...  100 us
    pallas_call x1, Pallas kernels, body(): pl.pallas_call(hand_out, out_shape=(jax.ShapeDtypeStruct(out.shape[1:], B...  2.45 us

profile of v3, /device:TPU:8, one launch (start us, length us, event | category | flops | bytes accessed | tf_op | source)
XLA Modules:
  0.0 103.2 jit_solution(12334221633352443216)
XLA Ops:
  0.6 100.1 %shard_map.120 = (bf16[2,3,32,256]{3,2,1,0:T(8,128)(2,1)}, f32[512,768]{1,0:T(8,128)}, f32[256,512]{1,0:T(8,128)}) custom-call(bf16[1,32,256]{2,1,0:T(8,128)(2,1)} %bitcast.16, bf16[2,32,256]{2,1,0:T(8,128)(2,1)} %bitcast.14, bf16[1,32,256]{2,1,0:T(8,128)(2,1)} %bitcast.17, bf16[2,32,256]{2,1,0:T(8,128)(2,1)} %bitcast.15, bf16[1,3,32,256]{3,2,1,0:T(8,128)(2,1)} %bitcast.13, ...), custom_call_target="tpu_custom_call" | custom-call | tf_op jit(solution)/shard_map/pallas_call | solution.py:452
  100.7 2.4 %shard_map.121 = (bf16[3,32,256]{2,1,0:T(8,128)(2,1)}, bf16[3,32,256]{2,1,0:T(8,128)(2,1)}, f32[512,768]{1,0:T(8,128)}, f32[256,512]{1,0:T(8,128)}) custom-call(bf16[2,3,32,256]{3,2,1,0:T(8,128)(2,1)} %get-tuple-element.11.out_ref, f32[512,768]{1,0:T(8,128)} %get-tuple-element.12.gq_ref, f32[256,512]{1,0:T(8,128)} %get-tuple-element.13.go_ref), custom_call_target="tpu_custom_call" | custom-call | tf_op jit(solution)/shard_map/pallas_call | solution.py:476

commit v4 on v3

--- a/solution.py
+++ b/solution.py
@@ -13,7 +13,8 @@
 HEAD_EPS = 1e-06
 TICKS = 3
 YS = 8
-COPIES = 352
+COPIES = 268
+POOL = 64
 BF = jnp.bfloat16
 F32 = jnp.float32
 
@@ -75,11 +76,18 @@
         loads.append(load)
 
     copies = []
+    drained = [0]
+
+    def drain(count):
+        for c in copies[drained[0]:count]:
+            c.wait_send()
+        drained[0] = count
 
     def send(src, dst, target):
         i = len(copies)
+        drain(max(drained[0], i - POOL + 1))
         c = pltpu.make_async_remote_copy(
-            src_ref=src, dst_ref=dst, send_sem=send_sems.at[i], recv_sem=recv_sems.at[i],
+            src_ref=src, dst_ref=dst, send_sem=send_sems.at[i % POOL], recv_sem=recv_sems.at[i],
             device_id=target, device_id_type=pl.DeviceIdType.MESH,
         )
         c.start()
@@ -189,8 +197,12 @@
             c, t = self.c, self.t
             for i in range(2):
                 self.passes[i].start(self.reduces[i].finish(), slot(c, t))
-                if i == (0 if t + 1 == TICKS else 1):
-                    outs.append((c, t, send(qown.at[c, t, 1 - z], qrecv.at[c, t], z_dev)))
+                if i == 0 and t + 1 == TICKS:
+                    self.swap()
+
+        def swap(self):
+            c, t = self.c, self.t
+            outs.append((c, t, send(qown.at[c, t, 1 - z], qrecv.at[c, t], z_dev)))
 
         def gather_start(self):
             for i in range(2):
@@ -232,13 +244,13 @@
         n32, _ = normed(slot(0, t))
         packed = mm(wt[...], n32.astype(BF)).astype(BF)
         mask = maskf[t]
-        mixed = []
-        for h in range(heads):
-            base = 3 * HD * h
-            q32, _ = head_norm(packed[base:base + HD].astype(F32))
-            k32, _ = head_norm(packed[base + HD:base + 2 * HD].astype(F32))
-            p = probs(q32.astype(BF), k32.astype(BF).T, mask)
-            mixed.append(mm(packed[base + 2 * HD:base + 3 * HD], p.astype(BF)).astype(BF))
+        hs = range(heads)
+        rows = [[packed[3 * HD * h + HD * i:3 * HD * h + HD * (i + 1)] for i in range(3)] for h in hs]
+        qn = [head_norm(rows[h][0].astype(F32))[0].astype(BF) for h in hs]
+        kn = [head_norm(rows[h][1].astype(F32))[0].astype(BF).T for h in hs]
+        w = [jnp.exp(mm(kn[h], qn[h]) * SCALE) * mask for h in hs]
+        p = [(w[h] * (1.0 / jnp.sum(w[h], axis=0, keepdims=True))).astype(BF) for h in hs]
+        mixed = [mm(rows[h][2], p[h]).astype(BF) for h in hs]
         term = mm(wot[...], jnp.concatenate(mixed, axis=0))
         part[0, t] = term.astype(BF).reshape(2, YS, 32, toks)
 
@@ -268,21 +280,23 @@
     def norm_back(grad, unit, factor):
         return factor * (grad - unit * jnp.mean(grad * unit, axis=0, keepdims=True))
 
-    def back_head(t, h):
+    def back_heads(t):
+        hs = range(heads)
         g = full[slot(1, t)].reshape(feat, toks)
-        dm = mm(wo_ref[h * HD:(h + 1) * HD], g).astype(BF)
-        dp = mm(v_s[t, h], dm)
-        base = 3 * HD * h
-        pb = pb_s[t, h]
-        dp_s[t, base + 2 * HD:base + 3 * HD] = mm_nt(dm, pb).astype(BF)
-        p = p_s[t, h]
-        pd = p * dp
-        inner = jnp.sum(pd, axis=0, keepdims=True)
-        ds = ((pd - p * inner) * SCALE).astype(BF)
-        dq = mm(kn_s[t, h], ds)
-        dk = mm_nt(qn_s[t, h], ds)
-        dp_s[t, base:base + HD] = norm_back(dq, q32_s[t, h], fac_s[t, h, 0:1]).astype(BF)
-        dp_s[t, base + HD:base + 2 * HD] = norm_back(dk, k32_s[t, h], fac_s[t, h, 1:2]).astype(BF)
+        dm = mm(wo_ref[...], g).astype(BF)
+        dm = [dm[h * HD:(h + 1) * HD] for h in hs]
+        dp = [mm(v_s[t, h], dm[h]) for h in hs]
+        pd = [p_s[t, h] * dp[h] for h in hs]
+        inner = [jnp.sum(pd[h], axis=0, keepdims=True) for h in hs]
+        ds = [((pd[h] - p_s[t, h] * inner[h]) * SCALE).astype(BF) for h in hs]
+        dv = [mm_nt(dm[h], pb_s[t, h]) for h in hs]
+        dq = [mm(kn_s[t, h], ds[h]) for h in hs]
+        dk = [mm_nt(qn_s[t, h], ds[h]) for h in hs]
+        for h in hs:
+            base = 3 * HD * h
+            dp_s[t, base + 2 * HD:base + 3 * HD] = dv[h].astype(BF)
+            dp_s[t, base:base + HD] = norm_back(dq[h], q32_s[t, h], fac_s[t, h, 0:1]).astype(BF)
+            dp_s[t, base + HD:base + 2 * HD] = norm_back(dk[h], k32_s[t, h], fac_s[t, h, 1:2]).astype(BF)
 
     def back_term(t):
         dn = mm(w_ref[...], dp_s[t])
@@ -302,15 +316,14 @@
             go_ref[...] += go
 
     def backward(t):
-        for h in range(heads):
-            back_head(t, h)
+        back_heads(t)
         back_term(t)
 
     for load in loads[:3]:
         load.wait()
     pl.semaphore_wait(barrier, len(partners))
 
-    order = [slot(2, 0), slot(1, 0), slot(0, 0)]
+    order = [slot(0, 0), slot(2, 0), slot(1, 0)]
     across = {}
     for b in order + [slot(2, 1), slot(2, 2)]:
         across[b] = send(full.at[b, z, y], full.at[b, z, y], z_dev)
@@ -336,40 +349,49 @@
         g.finish()
     for g in others:
         g.mid()
-    others[0].finish()
-    recompute(0)
-    others[1].finish()
 
     for t in range(TICKS):
         last = t + 1 == TICKS
         if t > 0:
             old_f, old_b = chain_f, chain_b
+            old_f.gather_finish()
+            forward(t)
+        chain_f, chain_b = Chain(0, t), Chain(1, t)
+        count = len(copies)
+        if t == 0:
+            others[0].finish()
+            forward(0)
+            chain_f.reduce_start()
+            others[1].finish()
+            recompute(0)
+            others[2].finish()
+        else:
+            chain_f.reduce_start()
             old_b.gather_finish()
         backward(t)
-        chain_f, chain_b = Chain(0, t), Chain(1, t)
         chain_b.reduce_start()
-        if t == 0:
-            others[2].finish()
-        else:
-            old_f.gather_finish()
-        forward(t)
-        chain_f.reduce_start()
         weight_terms(t)
+        drain(count)
+        chain_f.reduce_mid()
         chain_b.reduce_mid()
-        chain_f.reduce_mid()
+        count = len(copies)
+        chain_f.hand_over()
         chain_b.hand_over()
-        chain_f.hand_over()
         if not last:
             across[slot(2, t + 1)].wait_recv()
             kept = [Gather(slot(2, t + 1), h) for h in range(2)]
             for g in kept:
                 g.start()
+        drain(count)
+        if not last:
+            chain_f.gather_start()
             chain_b.gather_start()
-            chain_f.gather_start()
+            chain_f.swap()
+            chain_b.swap()
             for g in kept:
                 g.mid()
+            chain_f.gather_mid()
             chain_b.gather_mid()
-            chain_f.gather_mid()
             for g in kept:
                 g.finish()
             recompute(t + 1)
@@ -377,8 +399,7 @@
     for c, t, copy in outs:
         copy.wait_recv()
         out_ref[c, t] = (qown[c, t, z].astype(F32) + qrecv[c, t].astype(F32)).astype(BF)
-    for c in copies:
-        c.wait_send()
+    drain(len(copies))
 
 
 def hand_out(out_ref, gq_ref, go_ref, codes, grads, gq, go, out_v, gq_v, go_v, sems):
@@ -446,7 +467,7 @@
         pltpu.VMEM((TICKS, 1, toks), F32),
         pltpu.VMEM((TICKS, cols, toks), BF),
         pltpu.SemaphoreType.DMA((9,)),
-        pltpu.SemaphoreType.DMA((COPIES,)),
+        pltpu.SemaphoreType.DMA((POOL,)),
         pltpu.SemaphoreType.DMA((COPIES,)),
     ]
     out, gq, go = pl.pallas_call(

time: 103 us -> 98 us (0.951)
  Pallas kernels: 103 us -> 97.2 us
    pallas_call x1, Pallas kernels: 100 us -> 94.7 us  [body(): pl.pallas_call(functools.partial(kernel, sections), out_shape=(jax.ShapeD...]
where the time goes in v4:
time: 98 us; the launch traced here: 97.8 us
  Pallas kernels  97.2 us (99%)
    pallas_call x1, Pallas kernels, body(): pl.pallas_call(functools.partial(kernel, sections), out_shape=(jax.ShapeD...  94.7 us
    pallas_call x1, Pallas kernels, body(): pl.pallas_call(hand_out, out_shape=(jax.ShapeDtypeStruct(out.shape[1:], B...  2.45 us

profile of v4, /device:TPU:8, one launch (start us, length us, event | category | flops | bytes accessed | tf_op | source)
XLA Modules:
  0.0 97.8 jit_solution(1225234088820012243)
XLA Ops:
  0.6 94.7 %shard_map.120 = (bf16[2,3,32,256]{3,2,1,0:T(8,128)(2,1)}, f32[512,768]{1,0:T(8,128)}, f32[256,512]{1,0:T(8,128)}) custom-call(bf16[1,32,256]{2,1,0:T(8,128)(2,1)} %bitcast.16, bf16[2,32,256]{2,1,0:T(8,128)(2,1)} %bitcast.14, bf16[1,32,256]{2,1,0:T(8,128)(2,1)} %bitcast.17, bf16[2,32,256]{2,1,0:T(8,128)(2,1)} %bitcast.15, bf16[1,3,32,256]{3,2,1,0:T(8,128)(2,1)} %bitcast.13, ...), custom_call_target="tpu_custom_call" | custom-call | tf_op jit(solution)/shard_map/pallas_call | solution.py:473
  95.4 2.4 %shard_map.121 = (bf16[3,32,256]{2,1,0:T(8,128)(2,1)}, bf16[3,32,256]{2,1,0:T(8,128)(2,1)}, f32[512,768]{1,0:T(8,128)}, f32[256,512]{1,0:T(8,128)}) custom-call(bf16[2,3,32,256]{3,2,1,0:T(8,128)(2,1)} %get-tuple-element.11.out_ref, f32[512,768]{1,0:T(8,128)} %get-tuple-element.12.gq_ref, f32[256,512]{1,0:T(8,128)} %get-tuple-element.13.go_ref), custom_call_target="tpu_custom_call" | custom-call | tf_op jit(solution)/shard_map/pallas_call | solution.py:497

commit v5 on v4

--- a/solution.py
+++ b/solution.py
@@ -13,7 +13,7 @@
 HEAD_EPS = 1e-06
 TICKS = 3
 YS = 8
-COPIES = 268
+COPIES = 108
 POOL = 64
 BF = jnp.bfloat16
 F32 = jnp.float32
@@ -83,11 +83,19 @@
             c.wait_send()
         drained[0] = count
 
-    def send(src, dst, target):
+    single = [80]
+
+    def send(src, dst, target, base=None):
         i = len(copies)
+        if base is None:
+            arrival = single[0]
+            single[0] += 1
+        else:
+            arrival = base[0]
+            base[0] += 1
         drain(max(drained[0], i - POOL + 1))
         c = pltpu.make_async_remote_copy(
-            src_ref=src, dst_ref=dst, send_sem=send_sems.at[i % POOL], recv_sem=recv_sems.at[i],
+            src_ref=src, dst_ref=dst, send_sem=send_sems.at[i % POOL], recv_sem=recv_sems.at[arrival],
             device_id=target, device_id_type=pl.DeviceIdType.MESH,
         )
         c.start()
@@ -95,30 +103,31 @@
         return c
 
     class Gather:
-        def __init__(self, b, h):
+        def __init__(self, b, h, base):
+            self.base = [base]
             self.block = lambda k: full.at[b, h, at(k)]
             self.parts = lambda k, i: full.at[b, h, at(k), pl.ds(16 * i, 16)]
 
         def start(self):
             own = self.block(0)
-            self.two = [send(own, own, ring[2]), send(own, own, ring[-2])]
-            self.rest = [send(own, own, ring[1]), send(own, own, ring[-1])]
+            self.two = [send(own, own, ring[2], self.base), send(own, own, ring[-2], self.base)]
+            self.rest = [send(own, own, ring[1], self.base), send(own, own, ring[-1], self.base)]
 
         def mid(self):
             for i, d in enumerate((1, -1)):
                 self.two[i].wait_recv()
                 far = self.parts(-2 * d, i)
-                self.rest.append(send(far, far, ring[2 * d]))
+                self.rest.append(send(far, far, ring[2 * d], self.base))
                 block = self.block(-2 * d)
-                self.rest.append(send(block, block, ring[d]))
+                self.rest.append(send(block, block, ring[d], self.base))
 
         def finish(self):
             for c in self.rest:
                 c.wait_recv()
 
     class Reduce:
-        def __init__(self, c, t, h):
-            self.h = h
+        def __init__(self, c, t, h, base):
+            self.base = [base]
             self.p = part.at[c, t, h]
             self.r = rsb.at[c, t, h]
 
@@ -127,9 +136,9 @@
             self.first = []
             for i, d in enumerate((1, -1)):
                 rows = pl.ds(16 * i, 16)
-                far = send(p.at[at(4 * d), rows], r.at[i, 1, rows], ring[2 * d])
-                self.first.append((far, send(p.at[at(3 * d)], r.at[i, 0], ring[d])))
-            self.rest = [send(p.at[at(d)], r.at[i, 3], ring[d]) for i, d in enumerate((1, -1))]
+                far = send(p.at[at(4 * d), rows], r.at[i, 1, rows], ring[2 * d], self.base)
+                self.first.append((far, send(p.at[at(3 * d)], r.at[i, 0], ring[d], self.base)))
+            self.rest = [send(p.at[at(d)], r.at[i, 3], ring[d], self.base) for i, d in enumerate((1, -1))]
 
         def mid(self):
             p, r = self.p, self.r
@@ -141,7 +150,7 @@
                 none = jnp.zeros_like(far)
                 both = both + jnp.concatenate([far, none] if i == 0 else [none, far], axis=0)
                 r[i, 0] = both.astype(BF)
-                self.rest.append(send(r.at[i, 0], r.at[i, 2], ring[2 * d]))
+                self.rest.append(send(r.at[i, 0], r.at[i, 2], ring[2 * d], self.base))
 
         def finish(self):
             for c in self.rest:
@@ -181,9 +190,9 @@
         def __init__(self, c, t):
             self.c, self.t = c, t
             self.halves = (0, 1) if t + 1 < TICKS else (1 - z, z)
-            self.reduces = [Reduce(c, t, h) for h in self.halves]
+            self.reduces = [Reduce(c, t, h, 48 + 16 * c + 8 * i) for i, h in enumerate(self.halves)]
             self.passes = [Pass(c, t, h) for h in self.halves]
-            self.gathers = [Gather(slot(c, t + 1), h) for h in self.halves]
+            self.gathers = [Gather(slot(c, t + 1), h, 32 * c + 8 * i) for i, h in enumerate(self.halves)]
 
         def reduce_start(self):
             for r in self.reduces:
@@ -327,8 +336,8 @@
     across = {}
     for b in order + [slot(2, 1), slot(2, 2)]:
         across[b] = send(full.at[b, z, y], full.at[b, z, y], z_dev)
-    mine = [Gather(b, z) for b in order]
-    others = [Gather(b, 1 - z) for b in order]
+    mine = [Gather(b, z, 16 * i) for i, b in enumerate(order)]
+    others = [Gather(b, 1 - z, 16 * i + 8) for i, b in enumerate(order)]
     for g in mine:
         g.start()
     for load in loads[3:]:
@@ -379,7 +388,7 @@
         chain_b.hand_over()
         if not last:
             across[slot(2, t + 1)].wait_recv()
-            kept = [Gather(slot(2, t + 1), h) for h in range(2)]
+            kept = [Gather(slot(2, t + 1), h, 16 + 8 * h) for h in range(2)]
             for g in kept:
                 g.start()
         drain(count)

time: 98 us -> 96.6 us (0.986)
  Pallas kernels: 97.2 us -> 95.8 us
    pallas_call x1, Pallas kernels: 94.7 us -> 93.3 us  [body(): pl.pallas_call(functools.partial(kernel, sections), out_shape=(jax.ShapeD...]
where the time goes in v5:
time: 96.6 us; the launch traced here: 96.4 us
  Pallas kernels  95.8 us (99%)
    pallas_call x1, Pallas kernels, body(): pl.pallas_call(functools.partial(kernel, sections), out_shape=(jax.ShapeD...  93.3 us
    pallas_call x1, Pallas kernels, body(): pl.pallas_call(hand_out, out_shape=(jax.ShapeDtypeStruct(out.shape[1:], B...  2.45 us

profile of v5, /device:TPU:8, one launch (start us, length us, event | category | flops | bytes accessed | tf_op | source)
XLA Modules:
  0.0 96.4 jit_solution(3985013655040015649)
XLA Ops:
  0.6 93.3 %shard_map.120 = (bf16[2,3,32,256]{3,2,1,0:T(8,128)(2,1)}, f32[512,768]{1,0:T(8,128)}, f32[256,512]{1,0:T(8,128)}) custom-call(bf16[1,32,256]{2,1,0:T(8,128)(2,1)} %bitcast.16, bf16[2,32,256]{2,1,0:T(8,128)(2,1)} %bitcast.14, bf16[1,32,256]{2,1,0:T(8,128)(2,1)} %bitcast.17, bf16[2,32,256]{2,1,0:T(8,128)(2,1)} %bitcast.15, bf16[1,3,32,256]{3,2,1,0:T(8,128)(2,1)} %bitcast.13, ...), custom_call_target="tpu_custom_call" | custom-call | tf_op jit(solution)/shard_map/pallas_call | solution.py:482
  93.9 2.4 %shard_map.121 = (bf16[3,32,256]{2,1,0:T(8,128)(2,1)}, bf16[3,32,256]{2,1,0:T(8,128)(2,1)}, f32[512,768]{1,0:T(8,128)}, f32[256,512]{1,0:T(8,128)}) custom-call(bf16[2,3,32,256]{3,2,1,0:T(8,128)(2,1)} %get-tuple-element.11.out_ref, f32[512,768]{1,0:T(8,128)} %get-tuple-element.12.gq_ref, f32[256,512]{1,0:T(8,128)} %get-tuple-element.13.go_ref), custom_call_target="tpu_custom_call" | custom-call | tf_op jit(solution)/shard_map/pallas_call | solution.py:506
